TPU v7x, 32 devices: a whole 2x2x4 slice. The times are simulated.
32 devices in a mesh: head: 4 (over y, core), blk: 8 (over z, x).
Axes of the slice: x: 2, y: 2, z: 4, core: 2. Of those that a mesh axis runs over, the one named last changes fastest.
Arguments:
- states: bfloat16 [8192, 4096], P('blk', 'head'), may hold values from -6 to 6
- qkv_weight: bfloat16 [3, 4096, 4096], P(None, None, 'head'), may hold values from -1 to 1
- norm_gains: bfloat16 [2, 4096], P(None, 'head'), may hold values from 0.5 to 2
- kv_cache: bfloat16 [2, 320, 64, 4096], P(None, 'blk', None, 'head'), may hold values from -300 to 300
- cached_len: int32 [8], replicated, may hold values from 1 to 2048, as said below
- old_table: int32 [8, 32], replicated, may hold values from -1 to 319, as said below
- new_table: int32 [8, 16], replicated, may hold values from 0 to 319, as said below
Outputs:
- attended: bfloat16 [8192, 4096], P('blk', 'head')
- updated_cache: bfloat16 [2, 320, 64, 4096], P(None, 'blk', None, 'head')
Inputs may be any that keep to these rules, and one draw needn't show every extreme that they name: `cached_len`: one request has exactly 2048 cached tokens. old_table[r, b] is d * 40 plus a local slot for the blocks b of request r below the ceiling of cached_len[r] / 64, and -1 beyond; block b of request r lies on blk index d = (o + b) mod 8, where o is the index of its block 0. New block j of request r lies on blk index (p + j // 2) mod 8, where p is the index of its block 0; no slot appears twice in old_table and new_table together.
All inputs are finite; a program needn't handle non-finite values.
Results may differ from a plain program's by a relative error of at most 0.014.
The roundings to bfloat16 on the way count: a program that leaves them out, or rounds other values in their place, can miss the bound.
Values may be sent and summed in bfloat16 or wider, within the bound.
A program may use at most 192 MiB of HBM per device.

v0:
```python
import jax
import jax.numpy as jnp
from jax import lax
from jax.sharding import PartitionSpec as P

D = 4096
HS = 128


rope_base = 500000.0
norm_eps = 1e-06


def swapped(block, axis, apart):
    count = lax.axis_size(axis)
    route = []
    for low in range(count):
        high = low | 1 << apart
        if high != low and high < count:
            route += [(low, high), (high, low)]
    return lax.ppermute(block, axis, route)


def rotate(values, positions, head_size):
    half_size = head_size // 2
    frequency = rope_base ** (-jnp.arange(half_size, dtype=jnp.float32) * 2.0 / head_size)
    angles = positions.astype(jnp.float32)[:, None] * frequency[None, :]
    cosine = jnp.cos(angles)[:, None, :]
    sine_part = jnp.sin(angles)[:, None, :]
    first_half = values[..., :half_size]
    second = values[..., half_size:]
    return jnp.concatenate(
        [first_half * cosine - second * sine_part, second * cosine + first_half * sine_part],
        axis=-1,
    )


def body(states, qkv_weight, norm_gains, kv_cache, cached_len, old_table, new_table):
    tok_rows = states.shape[0]
    half_rows = tok_rows // 2
    local_width = qkv_weight.shape[2]
    local_heads = local_width // HS
    groups = lax.axis_size("blk")
    slot_count = kv_cache.shape[1]
    block_len = kv_cache.shape[2]
    requests = cached_len.shape[0]
    group_size = groups // requests
    per_dev = old_table.shape[1] // groups
    my_index = lax.axis_index("blk")
    request = my_index // group_size
    member = my_index % group_size
    late_block = 2 * group_size - 1 - member
    projected = jnp.einsum(
        "tc,jcw->tjw",
        lax.all_gather(states, "head", axis=1, tiled=True),
        qkv_weight,
        preferred_element_type=jnp.float32,
    )
    queries = projected[:, 0]
    key_new = projected[:, 1]
    value_new = projected[:, 2]
    query_sq, key_sq = lax.psum(
        (jnp.sum(queries * queries, axis=1), jnp.sum(key_new * key_new, axis=1)), "head"
    )
    gains = norm_gains.astype(jnp.float32)
    queries = queries * lax.rsqrt(query_sq / D + norm_eps)[:, None] * gains[0]
    key_new = key_new * lax.rsqrt(key_sq / D + norm_eps)[:, None] * gains[1]
    half_ids = jnp.arange(half_rows, dtype=jnp.int32)
    token_offset = jnp.concatenate(
        [member * half_rows + half_ids, late_block * half_rows + half_ids]
    )
    positions = cached_len[request] + token_offset
    queries = (
        rotate(queries.reshape(tok_rows, local_heads, HS), positions, HS)
        .reshape(tok_rows, local_width)
        .astype(jnp.bfloat16)
    )
    key_new = (
        rotate(key_new.reshape(tok_rows, local_heads, HS), positions, HS)
        .reshape(tok_rows, local_width)
        .astype(jnp.bfloat16)
    )
    value_new = value_new.astype(jnp.bfloat16)
    fresh_kv = jnp.stack([key_new, value_new])
    blocks_dev = tok_rows // block_len
    half_blocks = blocks_dev // 2
    new_count = new_table.shape[1]
    fresh_blocks = fresh_kv.reshape(2, blocks_dev, block_len, local_width)
    targets = jnp.arange(groups, dtype=jnp.int32)
    pair_index = jnp.arange(2, dtype=jnp.int32)
    new_home = new_table[:, 0] // slot_count
    wanted_out = 2 * ((targets - new_home[request]) % groups)[:, None] + pair_index[None, :]
    out_half = wanted_out // half_blocks
    local_index = jnp.where(
        out_half == member,
        wanted_out - member * half_blocks,
        wanted_out - late_block * half_blocks + half_blocks,
    )
    usable = (out_half == member) | (out_half == late_block)
    picked = jnp.take(fresh_blocks, jnp.clip(local_index, 0, blocks_dev - 1).reshape(-1), axis=1)
    picked = picked.reshape(2, groups, 2, block_len, local_width)
    picked = jnp.where(usable[None, :, :, None, None], picked, jnp.zeros((), jnp.bfloat16))
    arrived = lax.all_to_all(picked, "blk", split_axis=1, concat_axis=1, tiled=True)
    source_req = targets // group_size
    source_member = targets % group_size
    source_late = 2 * group_size - 1 - source_member
    wanted_in = 2 * ((my_index - new_home[source_req]) % groups)[:, None] + pair_index[None, :]
    in_half = wanted_in // half_blocks
    valid_in = (in_half == source_member[:, None]) | (in_half == source_late[:, None])
    target_slot = (
        new_table[source_req[:, None], jnp.clip(wanted_in, 0, new_count - 1)]
        - my_index * slot_count
    )
    target_slot = jnp.where(valid_in, target_slot, slot_count)
    updated_cache = kv_cache.at[:, target_slot.reshape(-1)].set(
        arrived.reshape(2, groups * 2, block_len, local_width), mode="drop"
    )
    lengths_blocks = jnp.sum((old_table >= 0).astype(jnp.int32), axis=1)
    first_dev = old_table[:, 0] // slot_count
    target_req = targets // group_size
    c_index = jnp.broadcast_to(jnp.arange(per_dev, dtype=jnp.int32)[None, :], (groups, per_dev))
    block_index = ((my_index - first_dev[target_req]) % groups)[:, None] + groups * c_index
    present = block_index < lengths_blocks[target_req][:, None]
    slot_index = (
        old_table[target_req[:, None], jnp.clip(block_index, 0, old_table.shape[1] - 1)]
        - my_index * slot_count
    )
    slot_index = jnp.clip(slot_index, 0, slot_count - 1)
    outgoing = jnp.take(kv_cache, slot_index.reshape(-1), axis=1).reshape(
        2, groups, per_dev, block_len, local_width
    )
    outgoing = jnp.where(present[None, :, :, None, None], outgoing, jnp.zeros((), jnp.bfloat16))
    received = lax.all_to_all(outgoing, "blk", split_axis=1, concat_axis=1, tiled=True)
    c_received = jnp.arange(per_dev, dtype=jnp.int32)
    source_first = (targets - first_dev[request]) % groups
    block_recv = source_first[:, None] + groups * c_received[None, :]
    key_pos = (
        block_recv[:, :, None] * block_len + jnp.arange(block_len, dtype=jnp.int32)[None, None, :]
    )
    cached_mask = jnp.broadcast_to(
        (key_pos < cached_len[request]).reshape(1, -1), (tok_rows, key_pos.size)
    )
    cached_keys = received[0].reshape(-1, local_width)
    cached_values = received[1].reshape(-1, local_width)
    collected = fresh_kv
    for bit_number in range(group_size.bit_length() - 1):
        partner_new = swapped(collected, "blk", bit_number)
        lower_new = member // 2**bit_number % 2 == 0
        collected = jnp.where(
            lower_new,
            jnp.concatenate([collected, partner_new], axis=1),
            jnp.concatenate([partner_new, collected], axis=1),
        )
    member_ids = jnp.arange(group_size, dtype=jnp.int32)[:, None]
    group_ids = jnp.concatenate(
        [
            member_ids * half_rows + half_ids[None, :],
            (2 * group_size - 1 - member_ids) * half_rows + half_ids[None, :],
        ],
        axis=1,
    ).reshape(-1)
    group_mask = group_ids[None, :] <= token_offset[:, None]
    all_keys = jnp.concatenate([cached_keys, collected[0]], axis=0)
    all_values = jnp.concatenate([cached_values, collected[1]], axis=0)
    full_mask = jnp.concatenate([cached_mask, group_mask], axis=1)
    score_scale = HS ** (-0.5)

    def one_head(head_index):
        q_head = lax.dynamic_slice_in_dim(queries, head_index * HS, HS, 1)
        k_head = lax.dynamic_slice_in_dim(all_keys, head_index * HS, HS, 1)
        v_head = lax.dynamic_slice_in_dim(all_values, head_index * HS, HS, 1)
        scores = (
            jnp.einsum("qd,kd->qk", q_head, k_head, preferred_element_type=jnp.float32)
            * score_scale
        )
        scores = jnp.where(full_mask, scores, -jnp.inf)
        row_max = jnp.max(scores, axis=1, keepdims=True)
        weights = jnp.exp(scores - row_max)
        probabilities = (weights / jnp.sum(weights, axis=1, keepdims=True)).astype(jnp.bfloat16)
        return jnp.dot(probabilities, v_head, preferred_element_type=jnp.float32).astype(
            jnp.bfloat16
        )

    heads_out = lax.map(one_head, jnp.arange(local_heads, dtype=jnp.int32))
    attended = jnp.transpose(heads_out, (1, 0, 2)).reshape(tok_rows, local_width)
    return (attended, updated_cache)


def solution(mesh):
    return jax.shard_map(
        body,
        mesh=mesh,
        in_specs=(
            P("blk", "head"),
            P(None, None, "head"),
            P(None, "head"),
            P(None, "blk", None, "head"),
            P(),
            P(),
            P(),
        ),
        out_specs=(P("blk", "head"), P(None, "blk", None, "head")),
        check_vma=False,
    )
```

profile of v0, /device:TPU:0, one launch (start us, length us, event | category | flops | bytes accessed | tf_op | source)
XLA Modules:
  0.0 378.8 jit_solution(6212726946108016126)
XLA Ops:
  7.2 10.4 %copy.66 = bf16[2,40,64,1024]{3,2,1,0:T(8,128)(2,1)} copy(bf16[2,40,64,1024]{3,2,1,0:T(8,128)(2,1)} %param.12) | data formatting | bytes 20971520
  21.2 9.5 %gather_fusion.3 = bf16[32,2,64,1024]{3,2,1,0:T(8,128)(2,1)} fusion(bf16[2,40,64,1024]{3,2,1,0:T(8,128)(2,1)} %copy.66, s32[1024]{0:T(1024)S(1)} %pad_clamp_fusion.1), kind=kCustom, calls=%fused_computation.3 | custom fusion | bytes 16777344 | tf_op jit(solution)/shard_map/jit(_take)/gather | solution.py:129
  30.7 9.5 %copy.38 = bf16[2,32,64,1024]{3,2,1,0:T(8,128)(2,1)} copy(bf16[2,32,64,1024]{3,2,0,1:T(8,128)(2,1)} %bitcast.65) | data formatting | bytes 16777216 | tf_op jit(solution)/shard_map/jit(_take)/gather | solution.py:129
  40.3 7.9 %select_select_fusion = bf16[2,8,4,64,1024]{4,3,2,1,0:T(8,128)(2,1)} fusion(bf16[2,8,4,64,1024]{4,3,2,1,0:T(8,128)(2,1)} %bitcast.66, pred[8,4]{1,0:T(8,128)(4,1)S(1)} %compare_and_fusion.1, pred[8,4]{1,0:T(8,128)(4,1)S(1)} %add_compare_fusion.1), kind=kLoop, calls=%fused_computation.24 | loop fusion | flops 8388608 | bytes 16777280 | tf_op jit(solution)/shard_map/jit(_where)/select_n | solution.py:132
  48.2 8.6 %copy.39 = bf16[2,8,4,64,1024]{4,3,2,0,1:T(8,128)(2,1)} copy(bf16[2,8,4,64,1024]{4,3,2,1,0:T(8,128)(2,1)} %select_select_fusion) | data formatting | bytes 16777216 | tf_op jit(solution)/shard_map/jit(_where)/select_n | solution.py:132
  56.8 7.1 %all-to-all-start = ((bf16[2,8,4,64,1024]{4,3,2,0,1:T(8,128)(2,1)}), bf16[2,8,4,64,1024]{4,3,2,0,1:T(8,128)(2,1)}, u32[]{:S(2)}, u32[]{:S(2)}) async-start(bf16[2,8,4,64,1024]{4,3,2,0,1:T(8,128)(2,1)} %copy.39), calls=%async_computation | async-start | bytes 16777216 | tf_op jit(solution)/shard_map/all_to_all | solution.py:133
  70.3 3.1 multiply_cosine_fusion
  76.1 2.6 all-gather.2.cloned.1.call-done
  78.8 33.2 %fusion.10 = f32[1024,3,1024]{0,2,1:T(8,128)} fusion(bf16[3,4096,1024]{2,1,0:T(8,128)(2,1)} %param.10, bf16[1024,4096]{1,0:T(8,128)(2,1)} %all-gather.2.cloned.1.call-done), kind=kOutput, calls=%fused_computation.22 | convolution fusion | flops 25769803776 | bytes 46137344 | tf_op jit(solution)/shard_map/tc,jcw->tjw/dot_general | solution.py:53
  112.0 3.9 %slice.92 = bf16[1024,1,1024]{0,2,1:T(8,128)(2,1)} slice(f32[1024,3,1024]{0,2,1:T(8,128)} %fusion.10), slice={[0:1024], [2:3], [0:1024]} | slice | bytes 4194304 | tf_op jit(solution)/shard_map/slice | solution.py:61
  115.9 3.8 %slice_bitcast_fusion = bf16[1024,1024]{0,1:T(8,128)(2,1)} fusion(f32[1024,3,1024]{0,2,1:T(8,128)} %fusion.10), kind=kLoop, calls=%fused_computation.131 | loop fusion | bytes 4194304 | tf_op jit(solution)/shard_map/convert_element_type | solution.py:83
  119.7 3.9 %copy.41 = bf16[1024,1024]{1,0:T(8,128)(2,1)} copy(bf16[1024,1024]{0,1:T(8,128)(2,1)} %slice_bitcast_fusion) | data formatting | bytes 4194304 | tf_op jit(solution)/shard_map/convert_element_type | solution.py:83
  123.6 3.9 %copy.43 = bf16[1024,1,1024]{2,0,1:T(8,128)(2,1)} copy(bf16[1024,1,1024]{0,2,1:T(8,128)(2,1)} %slice.92) | data formatting | bytes 4194304 | tf_op jit(solution)/shard_map/convert_element_type | solution.py:83
  127.6 8.5 %multiply_reduce_fusion = (f32[1024]{0:T(1024)S(1)}, f32[1024]{0:T(1024)S(1)}, f32[1024,1,1024]{0,2,1:T(8,128)}, f32[1024,1,1024]{0,2,1:T(8,128)}) fusion(f32[1024,3,1024]{0,2,1:T(8,128)} %fusion.10), kind=kLoop, calls=%fused_computation.34 | loop fusion | flops 4192256 | bytes 16785408 | tf_op jit(solution)/shard_map/reduce_sum | solution.py:63
  136.0 5.4 %copy.40 = f32[1024,8,128]{2,1,0:T(8,128)} copy(f32[1024,8,128]{0,2,1:T(8,128)} %bitcast.72) | data formatting | bytes 8388608 | tf_op jit(solution)/shard_map/squeeze | solution.py:60
  141.4 6.6 %all-reduce = (f32[1024]{0:T(1024)S(1)}, f32[1024]{0:T(1024)S(1)}) all-reduce(f32[1024]{0:T(1024)S(1)} %get-tuple-element.41, f32[1024]{0:T(1024)S(1)} %get-tuple-element.40), channel_id=1, replica_groups=mesh['head'=4,'blk'=8] {'head'}, use_global_device_ids=true, to_apply=%region_1.2 | all-reduce | flops 2048 | bytes 16384 | tf_op jit(solution)/shard_map/psum | solution.py:62
  148.1 4.8 %multiply_multiply_fusion = f32[1024,8,128]{2,1,0:T(8,128)S(1)} fusion(f32[1024,8,128]{2,1,0:T(8,128)} %copy.40, f32[8,128]{1,0:T(8,128)S(1)} %bitcast.78, f32[1024]{0:T(1024)S(1)} %get-tuple-element.78), kind=kLoop, calls=%fused_computation.33 | loop fusion | flops 2097152 | bytes 8396800 | tf_op jit(solution)/shard_map/mul | solution.py:67
  154.6 2.5 maximum_convert_fusion
  157.0 4.2 %convert_element_type.66 = bf16[1,16,64,1024]{3,2,1,0:T(8,128)(2,1)} reshape(bf16[1024,8,128]{2,1,0:T(8,128)(2,1)} %maximum_convert_fusion) | data formatting | bytes 4194304 | tf_op jit(solution)/shard_map/convert_element_type | solution.py:81
  161.2 3.5 copy.51
  164.7 5.4 %copy.37 = f32[1024,8,128]{2,1,0:T(8,128)} copy(f32[1024,8,128]{0,2,1:T(8,128)} %bitcast.71) | data formatting | bytes 8388608 | tf_op jit(solution)/shard_map/squeeze | solution.py:59
  170.1 4.7 %multiply_multiply_fusion.1 = f32[1024,8,128]{2,1,0:T(8,128)S(1)} fusion(f32[1024,8,128]{2,1,0:T(8,128)} %copy.37, f32[8,128]{1,0:T(8,128)S(1)} %bitcast.77, f32[1024]{0:T(1024)S(1)} %get-tuple-element.79), kind=kLoop, calls=%fused_computation.37 | loop fusion | flops 2097152 | bytes 8396800 | tf_op jit(solution)/shard_map/mul | solution.py:66
  182.0 4.9 %gather_fusion.6 = bf16[16,2,64,1024]{3,2,1,0:T(8,128)(2,1)} fusion(bf16[2,16,64,1024]{3,2,1,0:T(8,128)(2,1)} %pad_maximum_fusion.2, s32[1024]{0:T(1024)S(1)} %pad_clamp_fusion), kind=kCustom, calls=%fused_computation.6 | custom fusion | bytes 8388672 | tf_op jit(solution)/shard_map/jit(_take)/gather | solution.py:100
  186.9 4.7 %select_select_fusion.1 = bf16[2,8,2,64,1024]{4,3,0,2,1:T(8,128)(2,1)} fusion(bf16[2,8,2,64,1024]{4,3,0,2,1:T(8,128)(2,1)} %bitcast.68, pred[8,2]{1,0:T(8,128)(4,1)S(1)} %get-tuple-element.77, pred[8,2]{1,0:T(8,128)(4,1)S(1)} %get-tuple-element.76), kind=kLoop, calls=%fused_computation.30 | loop fusion | flops 4194304 | bytes 8388640 | tf_op jit(solution)/shard_map/jit(_where)/select_n | solution.py:102
  191.6 55.4 %all-to-all-done = bf16[2,8,4,64,1024]{4,3,2,0,1:T(8,128)(2,1)} async-done(((bf16[2,8,4,64,1024]{4,3,2,0,1:T(8,128)(2,1)}), bf16[2,8,4,64,1024]{4,3,2,0,1:T(8,128)(2,1)}, u32[]{:S(2)}, u32[]{:S(2)}) %all-to-all-start) | async-done | bytes 8388640 | tf_op jit(solution)/shard_map/all_to_all | solution.py:133
  247.0 4.8 %all-to-all-start.1 = ((bf16[2,8,2,64,1024]{4,3,0,2,1:T(8,128)(2,1)}), bf16[2,8,2,64,1024]{4,3,0,2,1:T(8,128)(2,1)}, u32[]{:S(2)}, u32[]{:S(2)}) async-start(bf16[2,8,2,64,1024]{4,3,0,2,1:T(8,128)(2,1)} %select_select_fusion.1), calls=%async_computation.1 | async-start | bytes 8388608 | tf_op jit(solution)/shard_map/all_to_all | solution.py:103
  251.9 5.5 %fusion.36 = (bf16[1,8,4,64,1024]{4,3,2,0,1:T(8,128)(2,1)}, bf16[1,8,4,64,1024]{4,3,2,0,1:T(8,128)(2,1)S(1)}) fusion(bf16[2,8,4,64,1024]{4,3,2,0,1:T(8,128)(2,1)} %all-to-all-done), kind=kLoop, calls=%fused_computation.129 | loop fusion | bytes 16777216 | tf_op jit(solution)/shard_map/slice | solution.py:144
  257.4 5.5 %pad_maximum_fusion.1 = bf16[3072,1024]{1,0:T(8,128)(2,1)} fusion(bf16[1024,1024]{1,0:T(8,128)(2,1)S(1)} %copy-done.2, bf16[2048,1024]{1,0:T(8,128)(2,1)} %bitcast.70), kind=kLoop, calls=%fused_computation.26 | loop fusion | flops 12582912 | bytes 12582912 | tf_op jit(solution)/shard_map/concatenate | solution.py:164
  262.9 5.1 %pad_maximum_fusion = bf16[3072,1024]{1,0:T(8,128)(2,1)} fusion(bf16[1024,1024]{1,0:T(8,128)(2,1)} %bitcast.75, bf16[2048,1024]{1,0:T(8,128)(2,1)S(1)} %bitcast.69), kind=kLoop, calls=%fused_computation.25 | loop fusion | flops 12582912 | bytes 12582912 | tf_op jit(solution)/shard_map/concatenate | solution.py:163
  268.0 89.9 %while.10 = (s32[]{:T(128)}, bf16[8,1024,128]{2,1,0:T(8,128)(2,1)}, s32[8]{0:T(128)S(1)}, bf16[1024,1024]{1,0:T(8,128)(2,1)}, bf16[3072,1024]{1,0:T(8,128)(2,1)}...) while((s32[]{:T(128)}, bf16[8,1024,128]{2,1,0:T(8,128)(2,1)}, ...), condition=%wide.region_8.9_spmd, body=%wide.region_5.8_spmd.sunk | while | flops 1635907584 | bytes 43013304 | solution.py:184
  269.2 3.7 fusion.45
  274.8 4.4 %fusion.47 = bf16[8,1024,128]{2,1,0:T(8,128)(2,1)} fusion(bf16[8,1024,128]{2,1,0:T(8,128)(2,1)} %get-tuple-element.141, s32[]{:T(128)S(6)} %copy.56, f32[1024,3072]{1,0:T(8,128)S(1)} %get-tuple-element.127, f32[1024]{0:T(1024)S(1)} %fusion.46, f32[1024]{0:T(1024)S(1)} %get-tuple-element.128, bf16[3072,1024]{1,0:T(8,128)(2,1)} %get-tuple-element.157, ...), kind=kOutput, calls=%fused_computation.15.clone.1 | convolution fusion | flops 814874624 | bytes 13639688 | tf_op jit(solution)/shard_map/while/body/eval_jaxpr/dot_general | solution.py:180
  280.5 3.7 fusion.45
  286.1 4.4 %fusion.47 = bf16[8,1024,128]{2,1,0:T(8,128)(2,1)} fusion(bf16[8,1024,128]{2,1,0:T(8,128)(2,1)} %get-tuple-element.141, s32[]{:T(128)S(6)} %copy.56, f32[1024,3072]{1,0:T(8,128)S(1)} %get-tuple-element.127, f32[1024]{0:T(1024)S(1)} %fusion.46, f32[1024]{0:T(1024)S(1)} %get-tuple-element.128, bf16[3072,1024]{1,0:T(8,128)(2,1)} %get-tuple-element.157, ...), kind=kOutput, calls=%fused_computation.15.clone.1 | convolution fusion | flops 814874624 | bytes 13639688 | tf_op jit(solution)/shard_map/while/body/eval_jaxpr/dot_general | solution.py:180
  291.7 3.7 fusion.45
  297.3 4.4 %fusion.47 = bf16[8,1024,128]{2,1,0:T(8,128)(2,1)} fusion(bf16[8,1024,128]{2,1,0:T(8,128)(2,1)} %get-tuple-element.141, s32[]{:T(128)S(6)} %copy.56, f32[1024,3072]{1,0:T(8,128)S(1)} %get-tuple-element.127, f32[1024]{0:T(1024)S(1)} %fusion.46, f32[1024]{0:T(1024)S(1)} %get-tuple-element.128, bf16[3072,1024]{1,0:T(8,128)(2,1)} %get-tuple-element.157, ...), kind=kOutput, calls=%fused_computation.15.clone.1 | convolution fusion | flops 814874624 | bytes 13639688 | tf_op jit(solution)/shard_map/while/body/eval_jaxpr/dot_general | solution.py:180
  302.9 3.7 fusion.45
  308.5 4.4 %fusion.47 = bf16[8,1024,128]{2,1,0:T(8,128)(2,1)} fusion(bf16[8,1024,128]{2,1,0:T(8,128)(2,1)} %get-tuple-element.141, s32[]{:T(128)S(6)} %copy.56, f32[1024,3072]{1,0:T(8,128)S(1)} %get-tuple-element.127, f32[1024]{0:T(1024)S(1)} %fusion.46, f32[1024]{0:T(1024)S(1)} %get-tuple-element.128, bf16[3072,1024]{1,0:T(8,128)(2,1)} %get-tuple-element.157, ...), kind=kOutput, calls=%fused_computation.15.clone.1 | convolution fusion | flops 814874624 | bytes 13639688 | tf_op jit(solution)/shard_map/while/body/eval_jaxpr/dot_general | solution.py:180
  314.2 3.7 fusion.45
  319.8 4.4 %fusion.47 = bf16[8,1024,128]{2,1,0:T(8,128)(2,1)} fusion(bf16[8,1024,128]{2,1,0:T(8,128)(2,1)} %get-tuple-element.141, s32[]{:T(128)S(6)} %copy.56, f32[1024,3072]{1,0:T(8,128)S(1)} %get-tuple-element.127, f32[1024]{0:T(1024)S(1)} %fusion.46, f32[1024]{0:T(1024)S(1)} %get-tuple-element.128, bf16[3072,1024]{1,0:T(8,128)(2,1)} %get-tuple-element.157, ...), kind=kOutput, calls=%fused_computation.15.clone.1 | convolution fusion | flops 814874624 | bytes 13639688 | tf_op jit(solution)/shard_map/while/body/eval_jaxpr/dot_general | solution.py:180
  325.4 3.7 fusion.45
  331.0 4.4 %fusion.47 = bf16[8,1024,128]{2,1,0:T(8,128)(2,1)} fusion(bf16[8,1024,128]{2,1,0:T(8,128)(2,1)} %get-tuple-element.141, s32[]{:T(128)S(6)} %copy.56, f32[1024,3072]{1,0:T(8,128)S(1)} %get-tuple-element.127, f32[1024]{0:T(1024)S(1)} %fusion.46, f32[1024]{0:T(1024)S(1)} %get-tuple-element.128, bf16[3072,1024]{1,0:T(8,128)(2,1)} %get-tuple-element.157, ...), kind=kOutput, calls=%fused_computation.15.clone.1 | convolution fusion | flops 814874624 | bytes 13639688 | tf_op jit(solution)/shard_map/while/body/eval_jaxpr/dot_general | solution.py:180
  336.7 3.7 fusion.45
  342.3 4.4 %fusion.47 = bf16[8,1024,128]{2,1,0:T(8,128)(2,1)} fusion(bf16[8,1024,128]{2,1,0:T(8,128)(2,1)} %get-tuple-element.141, s32[]{:T(128)S(6)} %copy.56, f32[1024,3072]{1,0:T(8,128)S(1)} %get-tuple-element.127, f32[1024]{0:T(1024)S(1)} %fusion.46, f32[1024]{0:T(1024)S(1)} %get-tuple-element.128, bf16[3072,1024]{1,0:T(8,128)(2,1)} %get-tuple-element.157, ...), kind=kOutput, calls=%fused_computation.15.clone.1 | convolution fusion | flops 814874624 | bytes 13639688 | tf_op jit(solution)/shard_map/while/body/eval_jaxpr/dot_general | solution.py:180
  347.9 3.7 fusion.45
  353.5 4.4 %fusion.47 = bf16[8,1024,128]{2,1,0:T(8,128)(2,1)} fusion(bf16[8,1024,128]{2,1,0:T(8,128)(2,1)} %get-tuple-element.141, s32[]{:T(128)S(6)} %copy.56, f32[1024,3072]{1,0:T(8,128)S(1)} %get-tuple-element.127, f32[1024]{0:T(1024)S(1)} %fusion.46, f32[1024]{0:T(1024)S(1)} %get-tuple-element.128, bf16[3072,1024]{1,0:T(8,128)(2,1)} %get-tuple-element.157, ...), kind=kOutput, calls=%fused_computation.15.clone.1 | convolution fusion | flops 814874624 | bytes 13639688 | tf_op jit(solution)/shard_map/while/body/eval_jaxpr/dot_general | solution.py:180
  357.9 3.2 copy_bitcast_fusion.2
  361.1 10.9 %scatter_fusion = bf16[2,40,64,1024]{3,2,1,0:T(8,128)(2,1)} fusion(bf16[2,40,64,1024]{3,2,1,0:T(8,128)(2,1)} %copy.66, s32[16]{0:T(128)S(1)} %copy-done.10, bf16[16,2,64,1024]{3,2,1,0:T(8,128)(2,1)} %bitcast.26), kind=kCustom, calls=%fused_computation.7 | custom fusion | bytes 12582976 | tf_op jit(solution)/shard_map/scatter | solution.py:115
  (103 shorter events, 41.2 us)
Async XLA Ops:
  7.2 11.4 %copy-start = (s32[8,32]{1,0:T(8,128)S(1)}, s32[8,32]{1,0:T(8,128)}, u32[]{:S(2)}) copy-start(s32[8,32]{1,0:T(8,128)} %param.14) | copy-start | bytes 3076
  7.2 10.5 %copy-start.1 = (s32[8,16]{1,0:T(8,128)S(1)}, s32[8,16]{1,0:T(8,128)}, u32[]{:S(2)}) copy-start(s32[8,16]{1,0:T(8,128)} %param.15) | copy-start | bytes 1540
  7.2 71.6 %all-gather.2.cloned.1.call-start = ((), (), s32[]{:S(2)}) async-start(), calls=%async_computation.2 | async-start | bytes 10485760 | tf_op jit(solution)/shard_map/all_gather | solution.py:55
  56.8 8.3 %copy-start.11 = (s32[8]{0:T(128)S(1)}, s32[8]{0:T(128)}, u32[]{:S(2)}) copy-start(s32[8]{0:T(128)} %param.13) | copy-start | bytes 100
  56.8 190.3 %all-to-all-start = ((bf16[2,8,4,64,1024]{4,3,2,0,1:T(8,128)(2,1)}), bf16[2,8,4,64,1024]{4,3,2,0,1:T(8,128)(2,1)}, u32[]{:S(2)}, u32[]{:S(2)}) async-start(bf16[2,8,4,64,1024]{4,3,2,0,1:T(8,128)(2,1)} %copy.39), calls=%async_computation | async-start | bytes 16777216 | tf_op jit(solution)/shard_map/all_to_all | solution.py:133
  63.9 6.4 %copy-start.9 = (bf16[2,1024]{1,0:T(2,128)(2,1)S(1)}, bf16[2,1024]{1,0:T(2,128)(2,1)}, u32[]{:S(2)}) copy-start(bf16[2,1024]{1,0:T(2,128)(2,1)} %param.11) | copy-start | bytes 12292
  148.0 4.8 %copy-start.5 = (f32[1024,64]{1,0:T(8,128)S(1)}, f32[1024,64]{1,0:T(8,128)}, u32[]{:S(2)}) copy-start(f32[1024,64]{1,0:T(8,128)} %get-tuple-element.70) | copy-start | bytes 786436
  148.1 4.8 %copy-start.7 = (f32[1024,64]{1,0:T(8,128)S(1)}, f32[1024,64]{1,0:T(8,128)}, u32[]{:S(2)}) copy-start(f32[1024,64]{1,0:T(8,128)} %get-tuple-element.71) | copy-start | bytes 786436
  170.1 4.7 %copy-start.6 = (f32[1024,64]{1,0:T(8,128)S(1)}, f32[1024,64]{1,0:T(8,128)}, u32[]{:S(2)}) copy-start(f32[1024,64]{1,0:T(8,128)} %get-tuple-element.70) | copy-start | bytes 786436
  170.1 4.8 %copy-start.8 = (f32[1024,64]{1,0:T(8,128)S(1)}, f32[1024,64]{1,0:T(8,128)}, u32[]{:S(2)}) copy-start(f32[1024,64]{1,0:T(8,128)} %get-tuple-element.71) | copy-start | bytes 786436
  176.6 3.1 copy-start.3
  176.6 3.1 copy-start.4
  247.0 114.1 %all-to-all-start.1 = ((bf16[2,8,2,64,1024]{4,3,0,2,1:T(8,128)(2,1)}), bf16[2,8,2,64,1024]{4,3,0,2,1:T(8,128)(2,1)}, u32[]{:S(2)}, u32[]{:S(2)}) async-start(bf16[2,8,2,64,1024]{4,3,0,2,1:T(8,128)(2,1)} %select_select_fusion.1), calls=%async_computation.1 | async-start | bytes 8388608 | tf_op jit(solution)/shard_map/all_to_all | solution.py:103
  251.9 5.5 %copy-start.2 = (bf16[1024,1024]{1,0:T(8,128)(2,1)S(1)}, bf16[1024,1024]{1,0:T(8,128)(2,1)}, u32[]{:S(2)}) copy-start(bf16[1024,1024]{1,0:T(8,128)(2,1)} %copy.41) | copy-start | bytes 6291460
  357.9 3.2 copy-start.10
Sparse Core Ops, SparseCore 0:
  17.7 60.9 all-gather.1
where the time goes:
time: 381 us; the launch traced here: 379 us
  local copies, waits for them, and re-layouts  109 us (29%)
  matrix products  98.3 us (26%)
  other arithmetic  75.5 us (20%)
  waiting for transfers between devices  58.1 us (15%)
  between operations  14.4 us (4%)
  starting transfers between devices  11.9 us (3%)
  blocking collectives  6.62 us (2%)
  loops' own time  5.22 us (1%)
    all_to_all x1, waiting for transfers between devices, body(): lax.all_to_all(outgoing, 'blk', split_axis=1, concat_axis=1, tiled=True)  55.4 us
    dot_general x8, matrix products, one_head(): jnp.dot(probabilities, v_head, preferred_element_type=jnp.float32)  35.1 us
    dot_general x1, matrix products, body(): jnp.einsum('tc,jcw->tjw', lax.all_gather(states, 'head', axis=1, tiled=Tr...  33.2 us
    dot_general x8, matrix products, one_head(): jnp.einsum('qd,kd->qk', q_head, k_head, preferred_element_type=jnp.float32)  30 us
    gather x2, local copies, waits for them, and re-layouts, body(): jnp.take(kv_cache, slot_index.reshape(-1), axis=1)  19 us
    unnamed x27, local copies, waits for them, and re-layouts  15.9 us
    reduce_sum x8, other arithmetic, one_head(): jnp.sum(weights, axis=1, keepdims=True)  14.8 us
    convert_element_type x3, local copies, waits for them, and re-layouts, body(): value_new = value_new.astype(jnp.bfloat16)  11.7 us
  transfers between devices with their start and end apart: 3, of which 2 were waited for; matrix products, arithmetic and copies ran while one was open for 69% of the time, Pallas kernels for 0%

commit v1 on v0

v1 whole, which is shorter than its diff:
```python
import functools

import jax
import jax.numpy as jnp
from jax import lax
from jax.experimental import pallas as pl
from jax.experimental.pallas import tpu as pltpu
from jax.sharding import PartitionSpec as P

D = 4096
HS = 128
PAIR = 2
NEAR = 2

rope_base = 500000.0
norm_eps = 1e-06
EXP2_SCALE = HS ** (-0.5) * 1.4426950408889634
LOW = -1e30
VMEM = 48 * 2**20


def swapped(block, axis, apart):
    count = lax.axis_size(axis)
    route = []
    for low in range(count):
        high = low | 1 << apart
        if high != low and high < count:
            route += [(low, high), (high, low)]
    return lax.ppermute(block, axis, route)


def pack_kernel(groups, group_size, slots, rounds, one, info, table, cache, near, far, sems):
    me = info[0]
    jobs = []
    for c in range(rounds):
        if c >= NEAR and one:
            jobs.append((c, info[1], far.at[c - NEAR]))
        else:
            for d in range(groups):
                ref = near.at[d, c] if c < NEAR else far.at[d, c - NEAR]
                jobs.append((c, d // group_size, ref))
    made = []
    for n, (c, r, ref) in enumerate(jobs):
        first = table[r, 0] // slots
        b = lax.rem(me - first + groups, groups) + groups * c
        entry = table[r, b]
        slot = jnp.clip(entry - me * slots, 0, slots - 1)
        copy = pltpu.make_async_copy(cache.at[:, slot], ref, sems.at[n])
        made.append((entry >= 0, copy))
        pl.when(entry >= 0)(copy.start)
    for there, copy in made:
        pl.when(there)(copy.wait)


def pack(kv_cache, info, old_table, groups, group_size, rounds, one):
    _, slots, length, width = kv_cache.shape
    near = (groups, NEAR, 2, length, width)
    far = (rounds - NEAR, 2, length, width)
    if not one:
        far = (groups,) + far
    hbm = pl.BlockSpec(memory_space=pl.ANY)
    return pl.pallas_call(
        functools.partial(pack_kernel, groups, group_size, slots, rounds, one),
        out_shape=[jax.ShapeDtypeStruct(near, jnp.bfloat16), jax.ShapeDtypeStruct(far, jnp.bfloat16)],
        grid_spec=pltpu.PrefetchScalarGridSpec(
            num_scalar_prefetch=2,
            grid=(1,),
            in_specs=[hbm],
            out_specs=[hbm, hbm],
            scratch_shapes=[pltpu.SemaphoreType.DMA((groups * rounds,))],
        ),
        name="pack",
    )(info, old_table, kv_cache)


def finish_kernel(heads, place, q_in, k_in, v_in, sums, gains, cosine, sine, q_out, k_out, sent):
    cos, sin = cosine[...], sine[...]
    scale = lax.rsqrt(sums[...] / D + norm_eps)
    for n, (raw, out) in enumerate(((q_in, q_out), (k_in, k_out))):
        for h in range(heads):
            cols = pl.ds(h * HS, HS)
            x = raw[:, cols] * scale[:, n : n + 1] * gains[n : n + 1, cols].astype(jnp.float32)
            y = (x * cos + pltpu.roll(x, HS // 2, 1) * sin).astype(jnp.bfloat16)
            out[:, cols] = y
            if n == 1:
                sent[0, 0, :, cols] = y
    sent[0, 1] = v_in[...]


def finish(place, q_raw, k_raw, v_new, sums, gains, cosine, sine, groups, tile):
    rows, width = q_raw.shape
    row = lambda w: pl.BlockSpec((tile, w), lambda t, place: (t, 0))
    return pl.pallas_call(
        functools.partial(finish_kernel, width // HS),
        out_shape=[
            jax.ShapeDtypeStruct((rows, width), jnp.bfloat16),
            jax.ShapeDtypeStruct((rows, width), jnp.bfloat16),
            jax.ShapeDtypeStruct((groups, 2, tile, width), jnp.bfloat16),
        ],
        grid_spec=pltpu.PrefetchScalarGridSpec(
            num_scalar_prefetch=1,
            grid=(rows // tile,),
            in_specs=[
                row(width), row(width), row(width), row(2),
                pl.BlockSpec((2, width), lambda t, place: (0, 0)),
                row(HS), row(HS),
            ],
            out_specs=[
                row(width), row(width),
                pl.BlockSpec((1, 2, tile, width), lambda t, place: (place[t], 0, 0, 0)),
            ],
        ),
        compiler_params=pltpu.CompilerParams(vmem_limit_bytes=VMEM),
        cost_estimate=pl.CostEstimate(flops=10 * rows * width, bytes_accessed=20 * rows * width, transcendentals=0),
        name="finish",
    )(place, q_raw, k_raw, v_new, sums, gains, cosine, sine)


def attend_kernel(groups, rounds, pieces, half, length, info, q_ref, k_ref, v_ref, near, far, out, acc, top, total):
    cached, first = info[0], info[1]
    span = groups * length

    def step(q, k, v, mask):
        s = lax.dot_general(q, k, (((1,), (1,)), ((), ())), preferred_element_type=jnp.float32)
        if mask is not None:
            s = jnp.where(mask, s, LOW)
        old = top[...]
        new = jnp.maximum(old, jnp.max(s, axis=1, keepdims=True))
        p = jnp.exp2((s - new[:, :1]) * EXP2_SCALE)
        shrink = jnp.exp2((old - new) * EXP2_SCALE)
        total[...] = total[...] * shrink + jnp.sum(p, axis=1, keepdims=True)
        acc[...] = acc[...] * shrink + jnp.dot(
            p.astype(jnp.bfloat16), v, preferred_element_type=jnp.float32
        )
        top[...] = new

    for part in range(2):
        mine = info[2 + part]
        rows = pl.ds(part * half, half)
        top[...] = jnp.full_like(top, LOW)
        total[...] = jnp.zeros_like(total)
        acc[...] = jnp.zeros_like(acc)
        for piece in range(pieces):
            theirs = info[4 + piece]
            keys = pl.ds(piece * half, half)

            @pl.when(theirs < mine)
            def _():
                step(q_ref[rows, :], k_ref[keys, :], v_ref[keys, :], None)

            @pl.when(theirs == mine)
            def _():
                a = lax.broadcasted_iota(jnp.int32, (half, half), 0)
                b = lax.broadcasted_iota(jnp.int32, (half, half), 1)
                step(q_ref[rows, :], k_ref[keys, :], v_ref[keys, :], b <= a)

        for c in range(rounds):
            ref, at = (near, c) if c < NEAR else (far, c - NEAR)

            @pl.when(cached >= (c + 1) * span)
            def _():
                k = ref[:, at, 0].reshape(span, HS)
                v = ref[:, at, 1].reshape(span, HS)
                step(q_ref[rows, :], k, v, None)

            @pl.when((cached > c * span) & (cached < (c + 1) * span))
            def _():
                k = ref[:, at, 0].reshape(span, HS)
                v = ref[:, at, 1].reshape(span, HS)

                def seen(shape, axis):
                    i = lax.broadcasted_iota(jnp.int32, shape, axis)
                    block = lax.rem(i // length - first + groups, groups) + groups * c
                    return block * length + lax.rem(i, length) < cached

                v = jnp.where(seen((span, HS), 0), v, jnp.zeros_like(v))
                step(q_ref[rows, :], k, v, seen((half, span), 1))

        out[rows, :] = (acc[...] / total[...]).astype(jnp.bfloat16)


def attend(info, queries, keys, values, near, far):
    rows, width = queries.shape
    groups, _, _, length, _ = near.shape
    rounds = near.shape[1] + far.shape[1]
    half = rows // 2
    pieces = keys.shape[0] // half
    flat = lambda n: pl.BlockSpec((n, HS), lambda h, info: (0, h))
    pool = lambda a: pl.BlockSpec(a.shape[:4] + (HS,), lambda h, info: (0, 0, 0, 0, h))
    count = keys.shape[0] + rounds * groups * length
    return pl.pallas_call(
        functools.partial(attend_kernel, groups, rounds, pieces, half, length),
        out_shape=jax.ShapeDtypeStruct((rows, width), jnp.bfloat16),
        grid_spec=pltpu.PrefetchScalarGridSpec(
            num_scalar_prefetch=1,
            grid=(width // HS,),
            in_specs=[flat(rows), flat(keys.shape[0]), flat(keys.shape[0]), pool(near), pool(far)],
            out_specs=flat(rows),
            scratch_shapes=[pltpu.VMEM((half, HS), jnp.float32)] * 3,
        ),
        compiler_params=pltpu.CompilerParams(vmem_limit_bytes=VMEM),
        cost_estimate=pl.CostEstimate(
            flops=8 * rows * width * count, bytes_accessed=4 * width * count, transcendentals=rows * count * width // HS
        ),
        name="attend",
    )(info, queries, keys, values, near, far)


def place_kernel(groups, group_size, half_pairs, slots, length, me_ref, table, arrived, cache, out, sems):
    me = me_ref[0]
    made = []
    for s in range(groups):
        r, m = s // group_size, s % group_size
        home = table[r, 0] // slots
        pair = lax.rem(me - home + groups, groups)
        here = (pair // half_pairs == m) | (pair // half_pairs == 2 * group_size - 1 - m)
        for i in range(PAIR):
            slot = jnp.clip(table[r, PAIR * pair + i] - me * slots, 0, slots - 1)
            copy = pltpu.make_async_copy(
                arrived.at[s, :, pl.ds(i * length, length)], out.at[:, slot], sems.at[s * PAIR + i]
            )
            made.append((here, copy))
            pl.when(here)(copy.start)
    for here, copy in made:
        pl.when(here)(copy.wait)


def place_new(me, new_table, arrived, kv_cache, groups, group_size, half_pairs):
    _, slots, length, _ = kv_cache.shape
    hbm = pl.BlockSpec(memory_space=pl.ANY)
    return pl.pallas_call(
        functools.partial(place_kernel, groups, group_size, half_pairs, slots, length),
        out_shape=jax.ShapeDtypeStruct(kv_cache.shape, kv_cache.dtype),
        grid_spec=pltpu.PrefetchScalarGridSpec(
            num_scalar_prefetch=2,
            grid=(1,),
            in_specs=[hbm, hbm],
            out_specs=hbm,
            scratch_shapes=[pltpu.SemaphoreType.DMA((groups * PAIR,))],
        ),
        input_output_aliases={3: 0},
        name="place",
    )(me, new_table, arrived, kv_cache)


def run(one, states, qkv_weight, norm_gains, kv_cache, cached_len, old_table, new_table):
    tok_rows = states.shape[0]
    half_rows = tok_rows // 2
    width = qkv_weight.shape[2]
    groups = lax.axis_size("blk")
    slots, length = kv_cache.shape[1:3]
    group_size = groups // cached_len.shape[0]
    rounds = old_table.shape[1] // groups
    me = lax.axis_index("blk").astype(jnp.int32)
    request, member = me // group_size, me % group_size
    late = 2 * group_size - 1 - member

    longest = jnp.argmax(old_table[:, NEAR * groups] >= 0).astype(jnp.int32)
    near, far = pack(kv_cache, jnp.stack([me, longest]), old_table, groups, group_size, rounds, one)
    near = lax.all_to_all(near, "blk", split_axis=0, concat_axis=0, tiled=True)
    if one:
        far = lax.all_gather(far, "blk", axis=0, tiled=False)
    else:
        far = lax.all_to_all(far, "blk", split_axis=0, concat_axis=0, tiled=True)

    whole = lax.all_gather(states, "head", axis=1, tiled=True)
    mul = lambda n: jnp.dot(whole, qkv_weight[n], preferred_element_type=jnp.float32)
    k_raw, q_raw = mul(1), mul(0)
    v_new = mul(2).astype(jnp.bfloat16)
    sums = lax.psum(
        jnp.stack([jnp.sum(q_raw * q_raw, axis=1), jnp.sum(k_raw * k_raw, axis=1)]), "head"
    ).T

    half_ids = jnp.arange(half_rows, dtype=jnp.int32)
    offset = jnp.concatenate([member * half_rows + half_ids, late * half_rows + half_ids])
    frequency = rope_base ** (-jnp.arange(HS // 2, dtype=jnp.float32) * 2.0 / HS)
    angles = (cached_len[request] + offset).astype(jnp.float32)[:, None] * frequency[None, :]
    cosine, sine = jnp.cos(angles), jnp.sin(angles)
    cosine = jnp.concatenate([cosine, cosine], axis=1)
    sine = jnp.concatenate([-sine, sine], axis=1)

    tile = PAIR * length
    half_pairs = half_rows // tile
    steps = jnp.arange(half_pairs, dtype=jnp.int32)
    pair = jnp.concatenate([member * half_pairs + steps, late * half_pairs + steps])
    place = (new_table[request, 0] // slots + pair) % groups
    queries, k_new, sent = finish(place, q_raw, k_raw, v_new, sums, norm_gains, cosine, sine, groups, tile)
    arrived = lax.all_to_all(sent, "blk", split_axis=0, concat_axis=0, tiled=True)

    keys, values = k_new, v_new
    for bit in range(group_size.bit_length() - 1):
        lower = member // 2**bit % 2 == 0
        both = []
        for mine in (keys, values):
            other = swapped(mine, "blk", bit)
            both.append(
                jnp.where(lower, jnp.concatenate([mine, other]), jnp.concatenate([other, mine]))
            )
        keys, values = both
    order = [p for m in range(group_size) for p in (m, 2 * group_size - 1 - m)]
    info = jnp.concatenate(
        [
            jnp.stack([cached_len[request], old_table[request, 0] // slots, member, late]),
            jnp.array(order, jnp.int32),
        ]
    ).astype(jnp.int32)
    attended = attend(info, queries, keys, values, near, far)
    updated = place_new(me[None], new_table, arrived, kv_cache, groups, group_size, half_pairs)
    return attended, updated


def body(*args):
    old_table = args[5]
    reach = NEAR * lax.axis_size("blk")
    alone = jnp.sum((old_table[:, reach] >= 0).astype(jnp.int32)) <= 1
    return lax.cond(alone, functools.partial(run, True), functools.partial(run, False), *args)


def solution(mesh):
    return jax.shard_map(
        body,
        mesh=mesh,
        in_specs=(
            P("blk", "head"),
            P(None, None, "head"),
            P(None, "head"),
            P(None, "blk", None, "head"),
            P(),
            P(),
            P(),
        ),
        out_specs=(P("blk", "head"), P(None, "blk", None, "head")),
        check_vma=False,
    )
```

time: 381 us -> 517 us (1.36)
  Pallas kernels: 0 us -> 284 us
  local copies, waits for them, and re-layouts: 109 us -> 27 us
  other arithmetic: 75.5 us -> 6.86 us
  matrix products: 98.3 us -> 45.5 us
  blocking collectives: 6.62 us -> 31.1 us
  starting transfers between devices: 11.9 us -> 25.9 us
  waiting for transfers between devices: 58.1 us -> 69.6 us
    pallas_call x0 -> x4, Pallas kernels: none -> 284 us  [the longest x1 129 us: place_new(): pl.pallas_call(functools.partial(place_kernel, groups, group_size, half_p...]
    dot_general x17 -> x3, matrix products: 98.3 us -> 45.5 us  [run(): jnp.dot(whole, qkv_weight[n], preferred_element_type=jnp.float32)]
    gather x8 -> x0, local copies, waits for them, and re-layouts: 27.2 us -> none  [the longest x2 19 us: body(): jnp.take(kv_cache, slot_index.reshape(-1), axis=1)]
    psum x1, blocking collectives: 6.62 us -> 31.1 us  [run(): lax.psum(jnp.stack([jnp.sum(q_raw * q_raw, axis=1), jnp.sum(k_raw * k_raw...]
    reduce_sum x10 -> x1, other arithmetic: 23.4 us -> 0.7 us  [body(): alone = jnp.sum((old_table[:, reach] >= 0).astype(jnp.int32)) <= 1]
    convert_element_type x4 -> x0, local copies, waits for them, and re-layouts: 15.9 us -> none  [the longest x3 11.7 us: body(): value_new = value_new.astype(jnp.bfloat16)]
    concatenate x8 -> x1, other arithmetic: 14.7 us -> 0.34 us  [run(): cosine = jnp.concatenate([cosine, cosine], axis=1)]
    all_to_all x2, starting transfers between devices: 11.9 us -> 25.8 us  [the longest x1 21.1 us: run(): near = lax.all_to_all(near, 'blk', split_axis=0, concat_axis=0, tiled=True)]
  transfers between devices with their start and end apart: 3 -> 4, of which waited for: 2 -> 2; matrix products, arithmetic and copies ran while one was open for 69% -> 13% of each run, Pallas kernels for 0% -> 30%
where the time goes in v1:
time: 517 us; the launch traced here: 513 us
  Pallas kernels  284 us (55%)
  waiting for transfers between devices  69.6 us (13%)
  matrix products  45.5 us (9%)
  blocking collectives  31.1 us (6%)
  local copies, waits for them, and re-layouts  27 us (5%)
  starting transfers between devices  25.9 us (5%)
  between operations  15 us (3%)
  loops' own time  7.48 us (1%)
  other arithmetic  6.86 us (1%)
    pallas_call x1, Pallas kernels, place_new(): pl.pallas_call(functools.partial(place_kernel, groups, group_size, half_p...  129 us
    pallas_call x1, Pallas kernels, pack(): pl.pallas_call(functools.partial(pack_kernel, groups, group_size, slots,...  89.4 us
    pallas_call x1, Pallas kernels, attend(): pl.pallas_call(functools.partial(attend_kernel, groups, rounds, pieces, h...  55.9 us
    dot_general x3, matrix products, run(): jnp.dot(whole, qkv_weight[n], preferred_element_type=jnp.float32)  45.5 us
    all_to_all x1, waiting for transfers between devices, run(): near = lax.all_to_all(near, 'blk', split_axis=0, concat_axis=0, tiled=True)  36.8 us
    all_to_all x1, waiting for transfers between devices, run(): lax.all_to_all(sent, 'blk', split_axis=0, concat_axis=0, tiled=True)  31.4 us
    psum x1, blocking collectives, run(): lax.psum(jnp.stack([jnp.sum(q_raw * q_raw, axis=1), jnp.sum(k_raw * k_raw...  31.1 us
    all_to_all x1, starting transfers between devices, run(): near = lax.all_to_all(near, 'blk', split_axis=0, concat_axis=0, tiled=True)  21.1 us
  transfers between devices with their start and end apart: 4, of which 2 were waited for; matrix products, arithmetic and copies ran while one was open for 13% of the time, Pallas kernels for 30%

profile of v1, /device:TPU:0, one launch (start us, length us, event | category | flops | bytes accessed | tf_op | source)
XLA Modules:
  0.0 512.7 jit_solution(18159512693820208464)
XLA Ops:
  7.2 0.0 copy-start.10
  7.2 0.0 copy-start.11
  7.2 0.0 copy-start.8
  7.2 0.0 copy-start.9
  7.2 10.4 %copy.55 = bf16[2,40,64,1024]{3,2,1,0:T(8,128)(2,1)} copy(bf16[2,40,64,1024]{3,2,1,0:T(8,128)(2,1)} %param.14) | data formatting | bytes 20971520
  17.6 0.0 copy-done.8
  17.6 0.7 convert_reduce_fusion
  18.9 0.0 copy-done.10
  19.0 0.0 copy-done.11
  19.0 0.0 copy-done.9
  19.0 486.7 %conditional.1 = (bf16[1024,1024]{1,0:T(8,128)(2,1)}, bf16[2,40,64,1024]{3,2,1,0:T(8,128)(2,1)}) conditional(s32[]{:T(128)} %convert_element_type.28, (s32[8]{0:T(128)S(1)}, s32[8,32]{1,0:T(8,128)S(1)}, s32[2]{0:T(128)S(1)}, s32[8,16]{1,0:T(8,128)S(1)}, bf16[1024,1024]{1,0:T(8,128)(2,1)}, /*index=5*/bf16[3,4096,1024]{2,1,0:T(8,128)(2,1)}, ...), branch_computations={%region_1.6_spmd, %region_6.11_spmd} | conditional | flops 51555733504 | bytes 218178784 | solution.py:316
  22.2 0.0 all-gather.7.cloned.1.call-start
  22.2 0.7 all-gather.7.cloned.1.call-update
  22.9 0.2 fusion.30
  23.1 0.6 iota_reduce_fusion.1
  23.8 1.2 pad_add_fusion.1.info
  24.9 89.4 %pack.3 = (bf16[8,2,2,64,1024]{4,3,2,1,0:T(8,128)(2,1)}, bf16[2,2,64,1024]{3,2,1,0:T(8,128)(2,1)}) custom-call(s32[2]{0:T(128)} %pad_add_fusion.1.info, s32[8,32]{1,0:T(8,128)S(1)} %get-tuple-element.47.table, bf16[2,40,64,1024]{3,2,1,0:T(8,128)(2,1)} %get-tuple-element.91.cache), custom_call_target="tpu_custom_call" | custom-call | tf_op jit(solution)/shard_map/cond/branch_1_fun/pack/pallas_call | solution.py:62
  114.3 21.1 %all-to-all-start.3 = ((bf16[8,2,2,64,1024]{4,3,2,1,0:T(8,128)(2,1)}), bf16[8,2,2,64,1024]{4,3,2,1,0:T(8,128)(2,1)}, u32[]{:S(2)}, u32[]{:S(2)}) async-start(bf16[8,2,2,64,1024]{4,3,2,1,0:T(8,128)(2,1)} %get-tuple-element.57), calls=%async_computation.3 | async-start | bytes 8388608 | tf_op jit(solution)/shard_map/cond/branch_1_fun/all_to_all | solution.py:260
  135.5 0.0 all-gather.9.cloned.1.call-start
  135.5 0.7 all-gather.9.cloned.1.call-update
  136.2 0.5 fusion.35
  138.0 0.7 dynamic_slice.17
  139.3 0.1 and_select_fusion.1.place
  139.4 0.7 fusion.29
  140.1 1.9 fusion.28
  142.0 0.3 pad_maximum_fusion.3
  142.4 0.0 all-gather.7.cloned.1.call-done
  142.4 15.6 %multiply_reduce_fusion.2 = (f32[1024]{0:T(1024)S(1)}, f32[1024,1024]{0,1:T(8,128)}) fusion(bf16[1024,4096]{1,0:T(8,128)(2,1)} %all-gather.7.cloned.1.call-done, bf16[3,4096,1024]{2,1,0:T(8,128)(2,1)} %get-tuple-element.87), kind=kOutput, calls=%fused_computation.43 | convolution fusion | flops 8592030720 | bytes 20975616 | tf_op jit(solution)/shard_map/cond/branch_1_fun/dot_general | solution.py:267
  158.0 15.1 %multiply_reduce_fusion.3 = (f32[1024]{0:T(1024)S(1)}, f32[1024,1024]{0,1:T(8,128)}) fusion(bf16[1024,4096]{1,0:T(8,128)(2,1)} %all-gather.7.cloned.1.call-done, bf16[3,4096,1024]{2,1,0:T(8,128)(2,1)} %get-tuple-element.87), kind=kOutput, calls=%fused_computation.44 | convolution fusion | flops 8592030720 | bytes 20975616 | tf_op jit(solution)/shard_map/cond/branch_1_fun/dot_general | solution.py:267
  173.2 0.2 copy.46
  173.4 5.4 %copy.48.k_in = f32[1024,1024]{1,0:T(8,128)} copy(f32[1024,1024]{0,1:T(8,128)} %get-tuple-element.113) | data formatting | bytes 8388608 | tf_op jit(solution)/shard_map/cond/branch_1_fun/dot_general | solution.py:267
  178.8 5.4 %copy.47.q_in = f32[1024,1024]{1,0:T(8,128)} copy(f32[1024,1024]{0,1:T(8,128)} %get-tuple-element.115) | data formatting | bytes 8388608 | tf_op jit(solution)/shard_map/cond/branch_1_fun/dot_general | solution.py:267
  184.1 31.1 %psum.13.sums = f32[1024,2]{1,0:T(8,128)S(1)} all-reduce(f32[1024,2]{1,0:T(8,128)S(1)} %bitcast.60), channel_id=1, replica_groups=mesh['head'=4,'blk'=8] {'head'}, use_global_device_ids=true, to_apply=%region_9.9 | all-reduce | flops 2048 | bytes 16384 | tf_op jit(solution)/shard_map/cond/branch_1_fun/psum | solution.py:270
  215.2 14.8 %fusion.25.v_in.v_ref = bf16[1024,1024]{1,0:T(8,128)(2,1)} fusion(bf16[1024,4096]{1,0:T(8,128)(2,1)} %all-gather.7.cloned.1.call-done, bf16[3,4096,1024]{2,1,0:T(8,128)(2,1)} %get-tuple-element.87), kind=kOutput, calls=%fused_computation.45 | convolution fusion | flops 8590983168 | bytes 18874368 | tf_op jit(solution)/shard_map/cond/branch_1_fun/dot_general | solution.py:267
  230.0 10.1 %finish.3 = (bf16[1024,1024]{1,0:T(8,128)(2,1)S(1)}, bf16[1024,1024]{1,0:T(8,128)(2,1)S(1)}, bf16[8,2,128,1024]{3,2,1,0:T(8,128)(2,1)}) custom-call(s32[8]{0:T(128)S(1)} %and_select_fusion.1.place, f32[1024,1024]{1,0:T(8,128)} %copy.47.q_in, f32[1024,1024]{1,0:T(8,128)} %copy.48.k_in, bf16[1024,1024]{1,0:T(8,128)(2,1)} %fusion.25.v_in.v_ref, ...), custom_call_target="tpu_custom_call" | custom-call | flops 10485760 | bytes 20971520 | tf_op jit(solution)/shard_map/cond/branch_1_fun/finish/pallas_call | solution.py:93
  240.1 0.0 copy-start
  240.1 1.3 copy-done
  241.4 0.0 copy-start.2
  241.4 1.3 copy-done.2
  242.7 36.8 %all-to-all-done.3.near = bf16[8,2,2,64,1024]{4,3,2,1,0:T(8,128)(2,1)} async-done(((bf16[8,2,2,64,1024]{4,3,2,1,0:T(8,128)(2,1)}), bf16[8,2,2,64,1024]{4,3,2,1,0:T(8,128)(2,1)}, u32[]{:S(2)}, u32[]{:S(2)}) %all-to-all-start.3) | async-done | bytes 4194336 | tf_op jit(solution)/shard_map/cond/branch_1_fun/all_to_all | solution.py:260
  279.5 4.7 all-to-all-start.4
  284.2 0.6 fusion.34
  286.9 0.8 concatenate.33.info
  287.6 0.0 copy-done.1
  287.6 1.6 copy-done.3
  289.2 55.9 %attend.3 = bf16[1024,1024]{1,0:T(8,128)(2,1)} custom-call(s32[6]{0:T(128)S(1)} %concatenate.33.info, bf16[1024,1024]{1,0:T(8,128)(2,1)S(1)} %copy-done.1, bf16[1024,1024]{1,0:T(8,128)(2,1)S(1)} %copy-done.3, bf16[1024,1024]{1,0:T(8,128)(2,1)} %fusion.25.v_in.v_ref, bf16[8,2,2,64,1024]{4,3,2,1,0:T(8,128)(2,1)} %all-to-all-done.3.near, ...), custom_call_target="tpu_custom_call" | custom-call | flops 25769803776 | bytes 12582912 | tf_op jit(solution)/shard_map/cond/branch_1_fun/attend/pallas_call | solution.py:191
  345.2 31.4 %all-to-all-done.4.arrived = bf16[8,2,128,1024]{3,2,1,0:T(8,128)(2,1)} async-done(((bf16[8,2,128,1024]{3,2,1,0:T(8,128)(2,1)}), bf16[8,2,128,1024]{3,2,1,0:T(8,128)(2,1)}, u32[]{:S(2)}, u32[]{:S(2)}) %all-to-all-start.4) | async-done | bytes 4194336 | tf_op jit(solution)/shard_map/cond/branch_1_fun/all_to_all | solution.py:288
  376.5 128.9 %place.3 = bf16[2,40,64,1024]{3,2,1,0:T(8,128)(2,1)} custom-call(s32[1]{0:T(128)} %bitcast.26.me_ref, s32[8,16]{1,0:T(8,128)S(1)} %get-tuple-element.83.table, bf16[8,2,128,1024]{3,2,1,0:T(8,128)(2,1)} %all-to-all-done.4.arrived, bf16[2,40,64,1024]{3,2,1,0:T(8,128)(2,1)} %get-tuple-element.91.cache), custom_call_target="tpu_custom_call", output_to_operand_aliasing={{}: (3, {})} | custom-call | tf_op jit(solution)/shard_map/cond/branch_1_fun/place/pallas_call | solution.py:231
  (10 shorter events, 0.0 us)
Async XLA Ops:
  7.2 11.8 %copy-start.10 = (bf16[2,1024]{1,0:T(2,128)(2,1)S(1)}, bf16[2,1024]{1,0:T(2,128)(2,1)}, u32[]{:S(2)}) copy-start(bf16[2,1024]{1,0:T(2,128)(2,1)} %param.13) | copy-start | bytes 12292
  7.2 11.8 %copy-start.11 = (s32[8]{0:T(128)S(1)}, s32[8]{0:T(128)}, u32[]{:S(2)}) copy-start(s32[8]{0:T(128)} %param.15) | copy-start | bytes 100
  7.2 10.4 %copy-start.8 = (s32[8,32]{1,0:T(8,128)S(1)}, s32[8,32]{1,0:T(8,128)}, u32[]{:S(2)}) copy-start(s32[8,32]{1,0:T(8,128)} %param.16) | copy-start | bytes 3076
  7.2 11.8 %copy-start.9 = (s32[8,16]{1,0:T(8,128)S(1)}, s32[8,16]{1,0:T(8,128)}, u32[]{:S(2)}) copy-start(s32[8,16]{1,0:T(8,128)} %param.17) | copy-start | bytes 1540
  22.2 120.2 %all-gather.7.cloned.1.call-start = ((), (), s32[]{:S(2)}) async-start(), calls=%async_computation.6 | async-start | bytes 10485760 | tf_op jit(solution)/shard_map/cond/branch_1_fun/all_gather | solution.py:266
  114.3 165.2 %all-to-all-start.3 = ((bf16[8,2,2,64,1024]{4,3,2,1,0:T(8,128)(2,1)}), bf16[8,2,2,64,1024]{4,3,2,1,0:T(8,128)(2,1)}, u32[]{:S(2)}, u32[]{:S(2)}) async-start(bf16[8,2,2,64,1024]{4,3,2,1,0:T(8,128)(2,1)} %get-tuple-element.57), calls=%async_computation.3 | async-start | bytes 8388608 | tf_op jit(solution)/shard_map/cond/branch_1_fun/all_to_all | solution.py:260
  135.5 152.2 %all-gather.9.cloned.1.call-start = ((), (), s32[]{:S(2)}) async-start(), calls=%async_computation.7 | async-start | bytes 4718592 | tf_op jit(solution)/shard_map/cond/branch_1_fun/all_gather | solution.py:262
  240.1 1.3 copy-start
  241.4 1.3 copy-start.2
  279.5 8.1 %copy-start.1 = (bf16[1024,1024]{1,0:T(8,128)(2,1)S(1)}, bf16[1024,1024]{1,0:T(8,128)(2,1)}, u32[]{:S(2)}) copy-start(bf16[1024,1024]{1,0:T(8,128)(2,1)} %copy-done) | copy-start | bytes 6291460 | tf_op jit(solution)/shard_map/cond
  279.5 97.0 %all-to-all-start.4 = ((bf16[8,2,128,1024]{3,2,1,0:T(8,128)(2,1)}), bf16[8,2,128,1024]{3,2,1,0:T(8,128)(2,1)}, u32[]{:S(2)}, u32[]{:S(2)}) async-start(bf16[8,2,128,1024]{3,2,1,0:T(8,128)(2,1)} %get-tuple-element.59), calls=%async_computation.4 | async-start | bytes 8388608 | tf_op jit(solution)/shard_map/cond/branch_1_fun/all_to_all | solution.py:288
  287.6 1.6 copy-start.3
Sparse Core Ops, SparseCore 0:
  24.6 60.9 all-gather.6
  138.4 137.0 all-gather.8

commit v2 on v1

--- a/solution.py
+++ b/solution.py
@@ -29,48 +29,39 @@
     return lax.ppermute(block, axis, route)
 
 
-def pack_kernel(groups, group_size, slots, rounds, one, info, table, cache, near, far, sems):
-    me = info[0]
-    jobs = []
-    for c in range(rounds):
-        if c >= NEAR and one:
-            jobs.append((c, info[1], far.at[c - NEAR]))
-        else:
-            for d in range(groups):
-                ref = near.at[d, c] if c < NEAR else far.at[d, c - NEAR]
-                jobs.append((c, d // group_size, ref))
-    made = []
-    for n, (c, r, ref) in enumerate(jobs):
+def move_kernel(info, table, block, *rest):
+    rest[-1][...] = block[...].reshape(rest[-1].shape)
+
+
+def pack_rounds(kv_cache, info, old_table, groups, group_size, start, stop, one):
+    _, slots, length, width = kv_cache.shape
+    count = stop - start
+    places = 1 if one else groups
+
+    def source(d, c, info, table):
+        r = info[1] if one else d // group_size
         first = table[r, 0] // slots
-        b = lax.rem(me - first + groups, groups) + groups * c
-        entry = table[r, b]
-        slot = jnp.clip(entry - me * slots, 0, slots - 1)
-        copy = pltpu.make_async_copy(cache.at[:, slot], ref, sems.at[n])
-        made.append((entry >= 0, copy))
-        pl.when(entry >= 0)(copy.start)
-    for there, copy in made:
-        pl.when(there)(copy.wait)
-
-
-def pack(kv_cache, info, old_table, groups, group_size, rounds, one):
-    _, slots, length, width = kv_cache.shape
-    near = (groups, NEAR, 2, length, width)
-    far = (rounds - NEAR, 2, length, width)
-    if not one:
-        far = (groups,) + far
-    hbm = pl.BlockSpec(memory_space=pl.ANY)
+        b = lax.rem(info[0] - first + groups, groups) + groups * (start + c)
+        return 0, jnp.clip(table[r, b] - info[0] * slots, 0, slots - 1), 0, 0
+
     return pl.pallas_call(
-        functools.partial(pack_kernel, groups, group_size, slots, rounds, one),
-        out_shape=[jax.ShapeDtypeStruct(near, jnp.bfloat16), jax.ShapeDtypeStruct(far, jnp.bfloat16)],
+        move_kernel,
+        out_shape=jax.ShapeDtypeStruct((places, count, 2, length, width), jnp.bfloat16),
         grid_spec=pltpu.PrefetchScalarGridSpec(
             num_scalar_prefetch=2,
-            grid=(1,),
-            in_specs=[hbm],
-            out_specs=[hbm, hbm],
-            scratch_shapes=[pltpu.SemaphoreType.DMA((groups * rounds,))],
-        ),
+            grid=(places, count),
+            in_specs=[pl.BlockSpec((2, 1, length, width), source)],
+            out_specs=pl.BlockSpec((1, 1, 2, length, width), lambda d, c, info, table: (d, c, 0, 0, 0)),
+        ),
+        compiler_params=pltpu.CompilerParams(vmem_limit_bytes=VMEM),
         name="pack",
     )(info, old_table, kv_cache)
+
+
+def pack(kv_cache, info, old_table, groups, group_size, rounds, one):
+    near = pack_rounds(kv_cache, info, old_table, groups, group_size, 0, NEAR, False)
+    far = pack_rounds(kv_cache, info, old_table, groups, group_size, NEAR, rounds, one)
+    return near, far[0] if one else far
 
 
 def finish_kernel(heads, place, q_in, k_in, v_in, sums, gains, cosine, sine, q_out, k_out, sent):
@@ -206,39 +197,35 @@
     )(info, queries, keys, values, near, far)
 
 
-def place_kernel(groups, group_size, half_pairs, slots, length, me_ref, table, arrived, cache, out, sems):
-    me = me_ref[0]
-    made = []
-    for s in range(groups):
-        r, m = s // group_size, s % group_size
-        home = table[r, 0] // slots
-        pair = lax.rem(me - home + groups, groups)
-        here = (pair // half_pairs == m) | (pair // half_pairs == 2 * group_size - 1 - m)
-        for i in range(PAIR):
-            slot = jnp.clip(table[r, PAIR * pair + i] - me * slots, 0, slots - 1)
-            copy = pltpu.make_async_copy(
-                arrived.at[s, :, pl.ds(i * length, length)], out.at[:, slot], sems.at[s * PAIR + i]
-            )
-            made.append((here, copy))
-            pl.when(here)(copy.start)
-    for here, copy in made:
-        pl.when(here)(copy.wait)
-
-
 def place_new(me, new_table, arrived, kv_cache, groups, group_size, half_pairs):
-    _, slots, length, _ = kv_cache.shape
-    hbm = pl.BlockSpec(memory_space=pl.ANY)
+    _, slots, length, width = kv_cache.shape
+    requests = new_table.shape[0]
+
+    def pair_of(r, me, table):
+        return lax.rem(me[0] - table[r, 0] // slots + groups, groups)
+
+    def source(r, i, me, table):
+        part = pair_of(r, me, table) // half_pairs
+        return r * group_size + jnp.minimum(part, 2 * group_size - 1 - part), 0, i, 0
+
+    def target(r, i, me, table):
+        slot = table[r, PAIR * pair_of(r, me, table) + i] - me[0] * slots
+        return 0, jnp.clip(slot, 0, slots - 1), 0, 0
+
     return pl.pallas_call(
-        functools.partial(place_kernel, groups, group_size, half_pairs, slots, length),
+        move_kernel,
         out_shape=jax.ShapeDtypeStruct(kv_cache.shape, kv_cache.dtype),
         grid_spec=pltpu.PrefetchScalarGridSpec(
             num_scalar_prefetch=2,
-            grid=(1,),
-            in_specs=[hbm, hbm],
-            out_specs=hbm,
-            scratch_shapes=[pltpu.SemaphoreType.DMA((groups * PAIR,))],
+            grid=(requests, PAIR),
+            in_specs=[
+                pl.BlockSpec((1, 2, length, width), source),
+                pl.BlockSpec(memory_space=pl.ANY),
+            ],
+            out_specs=pl.BlockSpec((2, 1, length, width), target),
         ),
         input_output_aliases={3: 0},
+        compiler_params=pltpu.CompilerParams(vmem_limit_bytes=VMEM),
         name="place",
     )(me, new_table, arrived, kv_cache)
 

time: 517 us -> 308 us (0.60)
  Pallas kernels: 284 us -> 88.6 us
  local copies, waits for them, and re-layouts: 27 us -> 43.2 us
  blocking collectives: 31.1 us -> 16.4 us
  starting transfers between devices: 25.9 us -> 12.1 us
  loops' own time: 7.48 us -> 13.2 us
    pallas_call x2 -> x3, Pallas kernels: 218 us -> 22.6 us  [the longest x2 11.6 us: pack_rounds(): pl.pallas_call(move_kernel, out_shape=jax.ShapeDtypeStruct((places, count...]
    all_to_all x1, waiting for transfers between devices: 36.8 us -> 0.01 us  [run(): near = lax.all_to_all(near, 'blk', split_axis=0, concat_axis=0, tiled=True)]
    all_gather x1, waiting for transfers between devices: 0.02 us -> 34.8 us  [run(): whole = lax.all_gather(states, 'head', axis=1, tiled=True)]
    all_to_all x1, starting transfers between devices: 21.1 us -> 6.32 us  [run(): near = lax.all_to_all(near, 'blk', split_axis=0, concat_axis=0, tiled=True)]
    psum x1, blocking collectives: 31.1 us -> 16.4 us  [run(): lax.psum(jnp.stack([jnp.sum(q_raw * q_raw, axis=1), jnp.sum(k_raw * k_raw...]
    dot_general x2, local copies, waits for them, and re-layouts: 10.7 us -> 24.9 us  [run(): jnp.dot(whole, qkv_weight[n], preferred_element_type=jnp.float32)]
    another operation x1, loops' own time: 7.48 us -> 13.2 us  [body(): lax.cond(alone, functools.partial(run, True), functools.partial(run, Fals...]
  transfers between devices with their start and end apart: 4 -> 4, of which waited for: 2 -> 2; matrix products, arithmetic and copies ran while one was open for 13% -> 25% of each run, Pallas kernels for 30% -> 25%
where the time goes in v2:
time: 308 us
  Pallas kernels  88.6 us (29%)
  waiting for transfers between devices  68.2 us (22%)
  matrix products  45 us (15%)
  local copies, waits for them, and re-layouts  43.2 us (14%)
  blocking collectives  16.4 us (5%)
  between operations  15 us (5%)
  loops' own time  13.2 us (4%)
  starting transfers between devices  12.1 us (4%)
  other arithmetic  6.34 us (2%)
    pallas_call x1, Pallas kernels, attend(): pl.pallas_call(functools.partial(attend_kernel, groups, rounds, pieces, h...  56 us
    dot_general x3, matrix products, run(): jnp.dot(whole, qkv_weight[n], preferred_element_type=jnp.float32)  45 us
    all_gather x1, waiting for transfers between devices, run(): whole = lax.all_gather(states, 'head', axis=1, tiled=True)  34.8 us
    all_to_all x1, waiting for transfers between devices, run(): lax.all_to_all(sent, 'blk', split_axis=0, concat_axis=0, tiled=True)  32.7 us
    dot_general x2, local copies, waits for them, and re-layouts, run(): jnp.dot(whole, qkv_weight[n], preferred_element_type=jnp.float32)  24.9 us
    psum x1, blocking collectives, run(): lax.psum(jnp.stack([jnp.sum(q_raw * q_raw, axis=1), jnp.sum(k_raw * k_raw...  16.4 us
    another operation x1, loops' own time, body(): lax.cond(alone, functools.partial(run, True), functools.partial(run, Fals...  13.2 us
    pallas_call x2, Pallas kernels, pack_rounds(): pl.pallas_call(move_kernel, out_shape=jax.ShapeDtypeStruct((places, count...  11.6 us
  transfers between devices with their start and end apart: 4, of which 2 were waited for; matrix products, arithmetic and copies ran while one was open for 25% of the time, Pallas kernels for 25%

profile of v2, /device:TPU:0, one launch (start us, length us, event | category | flops | bytes accessed | tf_op | source)
XLA Modules:
  0.0 308.0 jit_solution(10013085145636014004)
XLA Ops:
  7.2 0.0 copy-start.11
  7.2 0.0 copy-start.14
  7.2 0.0 copy-start.12
  7.2 0.0 copy-start.13
  7.2 10.4 %copy.55 = bf16[2,40,64,1024]{3,2,1,0:T(8,128)(2,1)} copy(bf16[2,40,64,1024]{3,2,1,0:T(8,128)(2,1)} %param.14) | data formatting | bytes 20971520
  17.6 0.0 copy-done.11
  17.6 0.7 convert_reduce_fusion
  19.0 0.0 copy-done.14
  19.0 0.0 copy-done.12
  19.0 0.0 copy-done.13
  19.0 282.0 %conditional.1 = (bf16[1024,1024]{1,0:T(8,128)(2,1)}, bf16[2,40,64,1024]{3,2,1,0:T(8,128)(2,1)}) conditional(s32[]{:T(128)} %convert_element_type.28, (s32[8]{0:T(128)S(1)}, s32[8,32]{1,0:T(8,128)S(1)}, s32[2]{0:T(128)S(1)}, s32[8,16]{1,0:T(8,128)S(1)}, bf16[1024,1024]{1,0:T(8,128)(2,1)}, /*index=5*/bf16[3,4096,1024]{2,1,0:T(8,128)(2,1)}, ...), branch_computations={%region_1.6_spmd, %region_6.11_spmd} | conditional | flops 51555733504 | bytes 250160400 | solution.py:303
  28.0 0.0 all-gather.6.cloned.1.call-start
  28.1 0.7 all-gather.6.cloned.1.call-update
  28.8 0.2 fusion.30
  29.0 0.7 iota_reduce_fusion.1
  29.6 0.6 pad_add_fusion.1.info
  30.3 9.2 %pack.6 = bf16[8,2,2,64,1024]{4,3,2,1,0:T(8,128)(2,1)S(1)} custom-call(s32[2]{0:T(128)S(1)} %pad_add_fusion.1.info, s32[8,32]{1,0:T(8,128)S(1)} %get-tuple-element.45.table, bf16[2,40,64,1024]{3,2,1,0:T(8,128)(2,1)} %get-tuple-element.87.block.rest_0_), custom_call_target="tpu_custom_call" | custom-call | tf_op jit(solution)/shard_map/cond/branch_1_fun/pack/pallas_call | solution.py:47
  39.5 0.0 copy-start
  39.5 2.1 copy-done
  41.6 6.3 %all-to-all-start.3 = ((bf16[8,2,2,64,1024]{4,3,2,1,0:T(8,128)(2,1)}), bf16[8,2,2,64,1024]{4,3,2,1,0:T(8,128)(2,1)}, u32[]{:S(2)}, u32[]{:S(2)}) async-start(bf16[8,2,2,64,1024]{4,3,2,1,0:T(8,128)(2,1)} %copy-done), calls=%async_computation.3 | async-start | bytes 8388608 | tf_op jit(solution)/shard_map/cond/branch_1_fun/all_to_all | solution.py:247
  47.9 0.0 all-gather.8.cloned.1.call-start
  47.9 2.4 pack.7
  50.4 0.0 all-gather.8.cloned.1.call-update
  50.4 0.6 fusion.35
  52.4 0.6 dynamic_slice.17
  53.7 0.1 and_select_fusion.1.place
  53.8 0.6 fusion.29
  54.4 1.9 fusion.28
  56.3 0.3 pad_maximum_fusion.3
  56.7 34.8 %all-gather.6.cloned.1.call-done = bf16[1024,4096]{1,0:T(8,128)(2,1)} async-done(((bf16[1024,1024]{1,0:T(8,128)(2,1)}), bf16[1024,4096]{1,0:T(8,128)(2,1)}) %all-gather.6.cloned.1.call-update) | async-done | bytes 8388624 | tf_op jit(solution)/shard_map/cond/branch_1_fun/all_gather | solution.py:253
  91.5 15.1 %multiply_reduce_fusion.3 = (f32[1024]{0:T(1024)S(1)}, f32[1024,1024]{0,1:T(8,128)}) fusion(bf16[1024,4096]{1,0:T(8,128)(2,1)} %all-gather.6.cloned.1.call-done, bf16[3,4096,1024]{2,1,0:T(8,128)(2,1)} %get-tuple-element.83), kind=kOutput, calls=%fused_computation.44 | convolution fusion | flops 8592030720 | bytes 20975616 | tf_op jit(solution)/shard_map/cond/branch_1_fun/dot_general | solution.py:254
  106.6 15.1 %multiply_reduce_fusion.2 = (f32[1024]{0:T(1024)S(1)}, f32[1024,1024]{0,1:T(8,128)}) fusion(bf16[1024,4096]{1,0:T(8,128)(2,1)} %all-gather.6.cloned.1.call-done, bf16[3,4096,1024]{2,1,0:T(8,128)(2,1)} %get-tuple-element.83), kind=kOutput, calls=%fused_computation.43 | convolution fusion | flops 8592030720 | bytes 20975616 | tf_op jit(solution)/shard_map/cond/branch_1_fun/dot_general | solution.py:254
  121.7 5.4 %copy.47.q_in = f32[1024,1024]{1,0:T(8,128)} copy(f32[1024,1024]{0,1:T(8,128)} %get-tuple-element.111) | data formatting | bytes 8388608 | tf_op jit(solution)/shard_map/cond/branch_1_fun/dot_general | solution.py:254
  127.1 19.6 %copy.48.k_in = f32[1024,1024]{1,0:T(8,128)} copy(f32[1024,1024]{0,1:T(8,128)} %get-tuple-element.109) | data formatting | bytes 8388608 | tf_op jit(solution)/shard_map/cond/branch_1_fun/dot_general | solution.py:254
  146.6 0.2 copy.46
  146.9 16.4 %psum.13.sums = f32[1024,2]{1,0:T(8,128)S(1)} all-reduce(f32[1024,2]{1,0:T(8,128)S(1)} %bitcast.59), channel_id=1, replica_groups=mesh['head'=4,'blk'=8] {'head'}, use_global_device_ids=true, to_apply=%region_9.9 | all-reduce | flops 2048 | bytes 16384 | tf_op jit(solution)/shard_map/cond/branch_1_fun/psum | solution.py:257
  163.3 14.8 %fusion.25.v_in.v_ref = bf16[1024,1024]{1,0:T(8,128)(2,1)} fusion(bf16[1024,4096]{1,0:T(8,128)(2,1)} %all-gather.6.cloned.1.call-done, bf16[3,4096,1024]{2,1,0:T(8,128)(2,1)} %get-tuple-element.83), kind=kOutput, calls=%fused_computation.45 | convolution fusion | flops 8590983168 | bytes 18874368 | tf_op jit(solution)/shard_map/cond/branch_1_fun/dot_general | solution.py:254
  178.1 10.1 %finish.3 = (bf16[1024,1024]{1,0:T(8,128)(2,1)S(1)}, bf16[1024,1024]{1,0:T(8,128)(2,1)S(1)}, bf16[8,2,128,1024]{3,2,1,0:T(8,128)(2,1)}) custom-call(s32[8]{0:T(128)S(1)} %and_select_fusion.1.place, f32[1024,1024]{1,0:T(8,128)} %copy.47.q_in, f32[1024,1024]{1,0:T(8,128)} %copy.48.k_in, bf16[1024,1024]{1,0:T(8,128)(2,1)} %fusion.25.v_in.v_ref, ...), custom_call_target="tpu_custom_call" | custom-call | flops 10485760 | bytes 20971520 | tf_op jit(solution)/shard_map/cond/branch_1_fun/finish/pallas_call | solution.py:84
  188.2 1.3 copy-done.3
  189.5 1.3 copy-done.5
  190.8 0.0 all-to-all-done.3.near
  190.8 5.7 %all-to-all-start.4 = ((bf16[8,2,128,1024]{3,2,1,0:T(8,128)(2,1)}), bf16[8,2,128,1024]{3,2,1,0:T(8,128)(2,1)}, u32[]{:S(2)}, u32[]{:S(2)}) async-start(bf16[8,2,128,1024]{3,2,1,0:T(8,128)(2,1)} %get-tuple-element.55), calls=%async_computation.4 | async-start | bytes 8388608 | tf_op jit(solution)/shard_map/cond/branch_1_fun/all_to_all | solution.py:275
  196.5 0.6 fusion.34
  198.9 0.7 concatenate.33.info
  199.6 1.6 copy-done.6
  201.2 56.0 %attend.3 = bf16[1024,1024]{1,0:T(8,128)(2,1)} custom-call(s32[6]{0:T(128)S(1)} %concatenate.33.info, bf16[1024,1024]{1,0:T(8,128)(2,1)S(1)} %copy-done.4, bf16[1024,1024]{1,0:T(8,128)(2,1)S(1)} %copy-done.6, bf16[1024,1024]{1,0:T(8,128)(2,1)} %fusion.25.v_in.v_ref, bf16[8,2,2,64,1024]{4,3,2,1,0:T(8,128)(2,1)} %all-to-all-done.3.near, ...), custom_call_target="tpu_custom_call" | custom-call | flops 25769803776 | bytes 12582912 | tf_op jit(solution)/shard_map/cond/branch_1_fun/attend/pallas_call | solution.py:182
  257.1 32.7 %all-to-all-done.4.block = bf16[8,2,128,1024]{3,2,1,0:T(8,128)(2,1)} async-done(((bf16[8,2,128,1024]{3,2,1,0:T(8,128)(2,1)}), bf16[8,2,128,1024]{3,2,1,0:T(8,128)(2,1)}, u32[]{:S(2)}, u32[]{:S(2)}) %all-to-all-start.4) | async-done | bytes 4194336 | tf_op jit(solution)/shard_map/cond/branch_1_fun/all_to_all | solution.py:275
  289.8 11.0 %place.3 = bf16[2,40,64,1024]{3,2,1,0:T(8,128)(2,1)} custom-call(s32[1]{0:T(128)} %bitcast.26.info, s32[8,16]{1,0:T(8,128)S(1)} %get-tuple-element.79.table, bf16[8,2,128,1024]{3,2,1,0:T(8,128)(2,1)} %all-to-all-done.4.block, bf16[2,40,64,1024]{3,2,1,0:T(8,128)(2,1)} %get-tuple-element.87.block.rest_0_), custom_call_target="tpu_custom_call", output_to_operand_aliasing={{}: (3, {})} | custom-call | tf_op jit(solution)/shard_map/cond/branch_1_fun/place/pallas_call | solution.py:215
  (13 shorter events, 0.0 us)
Async XLA Ops:
  7.2 10.4 %copy-start.11 = (s32[8,32]{1,0:T(8,128)S(1)}, s32[8,32]{1,0:T(8,128)}, u32[]{:S(2)}) copy-start(s32[8,32]{1,0:T(8,128)} %param.16) | copy-start | bytes 3076
  7.2 11.8 %copy-start.14 = (s32[8]{0:T(128)S(1)}, s32[8]{0:T(128)}, u32[]{:S(2)}) copy-start(s32[8]{0:T(128)} %param.15) | copy-start | bytes 100
  7.2 11.8 %copy-start.12 = (s32[8,16]{1,0:T(8,128)S(1)}, s32[8,16]{1,0:T(8,128)}, u32[]{:S(2)}) copy-start(s32[8,16]{1,0:T(8,128)} %param.17) | copy-start | bytes 1540
  7.2 11.8 %copy-start.13 = (bf16[2,1024]{1,0:T(2,128)(2,1)S(1)}, bf16[2,1024]{1,0:T(2,128)(2,1)}, u32[]{:S(2)}) copy-start(bf16[2,1024]{1,0:T(2,128)(2,1)} %param.13) | copy-start | bytes 12292
  28.0 63.4 %all-gather.6.cloned.1.call-start = ((), (), s32[]{:S(2)}) async-start(), calls=%async_computation.6 | async-start | bytes 10485760 | tf_op jit(solution)/shard_map/cond/branch_1_fun/all_gather | solution.py:253
  39.5 2.1 copy-start
  41.6 149.2 %all-to-all-start.3 = ((bf16[8,2,2,64,1024]{4,3,2,1,0:T(8,128)(2,1)}), bf16[8,2,2,64,1024]{4,3,2,1,0:T(8,128)(2,1)}, u32[]{:S(2)}, u32[]{:S(2)}) async-start(bf16[8,2,2,64,1024]{4,3,2,1,0:T(8,128)(2,1)} %copy-done), calls=%async_computation.3 | async-start | bytes 8388608 | tf_op jit(solution)/shard_map/cond/branch_1_fun/all_to_all | solution.py:247
  47.9 151.7 %all-gather.8.cloned.1.call-start = ((), (), s32[]{:S(2)}) async-start(), calls=%async_computation.7 | async-start | bytes 4718592 | tf_op jit(solution)/shard_map/cond/branch_1_fun/all_gather | solution.py:249
  188.2 1.3 copy-start.3
  189.5 1.3 copy-start.5
  190.8 8.8 %copy-start.4 = (bf16[1024,1024]{1,0:T(8,128)(2,1)S(1)}, bf16[1024,1024]{1,0:T(8,128)(2,1)}, u32[]{:S(2)}) copy-start(bf16[1024,1024]{1,0:T(8,128)(2,1)} %copy-done.3) | copy-start | bytes 6291460 | tf_op jit(solution)/shard_map/cond
  190.8 99.0 %all-to-all-start.4 = ((bf16[8,2,128,1024]{3,2,1,0:T(8,128)(2,1)}), bf16[8,2,128,1024]{3,2,1,0:T(8,128)(2,1)}, u32[]{:S(2)}, u32[]{:S(2)}) async-start(bf16[8,2,128,1024]{3,2,1,0:T(8,128)(2,1)} %get-tuple-element.55), calls=%async_computation.4 | async-start | bytes 8388608 | tf_op jit(solution)/shard_map/cond/branch_1_fun/all_to_all | solution.py:275
  199.6 1.6 copy-start.6
Sparse Core Ops, SparseCore 0:
  30.4 60.9 all-gather.5
  93.6 98.7 all-gather.7
